TPU v7x, 32 devices: a whole 2x2x4 slice. The times are simulated.
32 devices in a mesh: wide: 4 (over y, x), narrow: 8 (over z, core).
Axes of the slice: x: 2, y: 2, z: 4, core: 2. Of those that a mesh axis runs over, the one named last changes fastest.
Arguments:
- vectors: float32 [65536, 128], P(('wide', 'narrow')), may hold values from -24 to 24
- near_blocks: bfloat16 [128, 3, 512, 512], P(('wide', 'narrow')), may hold values from -0.15625 to 0.15625
- leaf_basis: bfloat16 [65536, 256], P(('wide', 'narrow')), may hold values from -0.125 to 0.125
- transfer: bfloat16 [32, 256, 256], P(('wide', 'narrow')), may hold values from -0.125 to 0.125
- leaf_coupling: bfloat16 [32, 6, 256, 256], P(('wide', 'narrow')), may hold values from -0.15625 to 0.15625
- leaf_partners: int32 [32, 6], P(('wide', 'narrow')), may hold values from 0 to 7, as said below
- parent_coupling: bfloat16 [4, 3, 256, 256], P('wide'), may hold values from -0.21875 to 0.21875
- parent_partners: int32 [4, 3], P('wide'), may hold values from 0 to 3, as said below
- shifts: float32 [128], replicated, may hold values from -1 to 1
Outputs:
- filtered: float32 [65536, 128], P(('wide', 'narrow'))
Inputs may be any that keep to these rules, and one draw needn't show every extreme that they name: `leaf_partners`: row l lists 6 different sibling indices, none equal to l mod 8. `parent_partners`: row p lists 3 different parent indices, none equal to p.
All inputs are finite; a program needn't handle non-finite values.
Results may differ from a plain program's by a relative error of at most 0.01.
Values may be sent and summed in bfloat16 or wider, within the bound.
A program may use at most 64 MiB of HBM per device.

v0:
```python
import jax
import jax.numpy as jnp
from jax import lax
from jax.sharding import PartitionSpec as P

BLK = 512
DEGREE = 3


def extended_2(cells, sides, width):
    for axis, dim in sides:
        count = lax.axis_size(axis)
        ends = count - 1
        head = lax.slice_in_dim(cells, 0, width, axis=dim)
        tail = lax.slice_in_dim(cells, cells.shape[dim] - width, cells.shape[dim], axis=dim)
        cells = jnp.concatenate(
            [
                lax.ppermute(tail, axis, [(i, (i + 1) % count) for i in range(ends)]),
                cells,
                lax.ppermute(head, axis, [((i + 1) % count, i) for i in range(ends)]),
            ],
            axis=dim,
        )
    return cells


def pick_fold(partners, piece):
    indices = jnp.arange(piece.shape[0], dtype=jnp.int32)
    select = (partners[:, None] == indices[None, :]).astype(jnp.bfloat16)
    return jnp.einsum("jm,mrv->jrv", select, piece, preferred_element_type=jnp.float32)


def shards(
    vectors,
    near_blocks,
    leaf_basis,
    transfer,
    leaf_coupling,
    leaf_partners,
    parent_coupling,
    parent_partners,
    shifts,
):
    local_rows = vectors.shape[0]
    count_blocks = local_rows // BLK
    columns = vectors.shape[1]

    def apply_operator(field):
        vin = field.astype(jnp.bfloat16)
        extended = extended_2(vin, ((("wide", "narrow"), 0),), BLK)
        fields = extended.reshape(count_blocks + 2, BLK, columns)
        near = jnp.einsum(
            "bij,bjv->biv", near_blocks[:, 0], fields[:-2], preferred_element_type=jnp.float32
        )
        near = near + jnp.einsum(
            "bij,bjv->biv", near_blocks[:, 1], fields[1:-1], preferred_element_type=jnp.float32
        )
        near = near + jnp.einsum(
            "bij,bjv->biv", near_blocks[:, 2], fields[2:], preferred_element_type=jnp.float32
        )
        near = near.reshape(local_rows, columns)
        coeff = lax.dot_general(
            leaf_basis, vin, (((0,), (0,)), ((), ())), preferred_element_type=jnp.float32
        )
        coeff_b = coeff.astype(jnp.bfloat16)
        picked = pick_fold(
            leaf_partners[0], lax.all_gather(coeff_b[None], "narrow", axis=0, tiled=True)
        )
        leaf_far = jnp.einsum(
            "jrs,jsv->rv",
            leaf_coupling[0],
            picked.astype(jnp.bfloat16),
            preferred_element_type=jnp.float32,
        )
        upward = lax.dot_general(
            transfer[0], coeff_b, (((0,), (0,)), ((), ())), preferred_element_type=jnp.float32
        )
        share = lax.psum_scatter(
            upward.astype(jnp.bfloat16), "narrow", scatter_dimension=1, tiled=True
        )
        top_in = share[None]
        gathered = pick_fold(parent_partners[0], lax.all_gather(top_in, "wide", axis=0, tiled=True))
        part_out = jnp.einsum(
            "jrs,jsv->rv",
            parent_coupling[0],
            gathered.astype(jnp.bfloat16),
            preferred_element_type=jnp.float32,
        ).astype(jnp.bfloat16)
        parent_out = lax.all_gather(part_out, "narrow", axis=1, tiled=True)
        downward = jnp.dot(transfer[0], parent_out, preferred_element_type=jnp.float32)
        far_coeff = (leaf_far + downward).astype(jnp.bfloat16)
        return near + jnp.dot(leaf_basis, far_coeff, preferred_element_type=jnp.float32)

    previous = vectors
    current = apply_operator(vectors) - shifts[None, :] * vectors
    for step in range(1, DEGREE):
        following = 2.0 * (apply_operator(current) - shifts[None, :] * current) - previous
        previous, current = (current, following)
    squares = lax.psum(jnp.sum(current * current, axis=0), ("wide", "narrow"))
    total_rows = local_rows * lax.axis_size("wide") * lax.axis_size("narrow")
    meansq = squares / total_rows
    return current / jnp.sqrt(meansq + 1e-06)[None, :]


def solution(mesh):
    return jax.shard_map(
        shards,
        mesh=mesh,
        in_specs=(
            P(("wide", "narrow"), None),
            P(("wide", "narrow"), None, None, None),
            P(("wide", "narrow"), None),
            P(("wide", "narrow"), None, None),
            P(("wide", "narrow"), None, None, None),
            P(("wide", "narrow"), None),
            P("wide", None, None, None),
            P("wide", None),
            P(),
        ),
        out_specs=P(("wide", "narrow"), None),
        check_vma=False,
    )
```

profile of v0, /device:TPU:0, one launch (start us, length us, event | category | flops | bytes accessed | tf_op | source)
XLA Modules:
  0.0 273.5 jit_solution(12849994066574184903)
XLA Ops:
  6.6 1.4 convert_element_type.96
  8.6 1.7 fusion.70
  11.1 3.0 %collective-permute-start = (bf16[512,128]{1,0:T(8,128)(2,1)}, bf16[512,128]{1,0:T(8,128)(2,1)}, u32[]{:S(2)}, u32[]{:S(2)}) collective-permute-start(bf16[512,128]{1,0:T(8,128)(2,1)} %get-tuple-element.15), channel_id=1, source_target_pairs={{0,1},{1,2},{2,3},{3,4},{4,5},{5,6},{6,7},{7,8},{8,9},{9,10},{10,1... | collective-permute-start | bytes 393224 | tf_op jit(solution)/shard_map/ppermute | solution.py:18
  14.1 1.3 collective-permute-start.1
  15.4 20.1 %all-gather = bf16[2048,128]{1,0:T(8,128)(2,1)} all-gather(bf16[256,128]{1,0:T(8,128)(2,1)S(1)} %convolution_convert_fusion.2), channel_id=2, replica_groups=mesh['wide'=4,'narrow'=8] {'narrow'}, dimensions={0}, use_global_device_ids=true | all-gather | bytes 589824 | tf_op jit(solution)/shard_map/all_gather | solution.py:67
  35.4 1.6 copy.33
  37.0 1.5 fusion.94
  38.5 3.4 %fusion.20 = f32[4,512,128]{1,2,0:T(8,128)} fusion(bf16[4,512,128]{2,1,0:T(8,128)(2,1)S(1)} %bitcast.246, bf16[4,3,512,512]{3,2,1,0:T(8,128)(2,1)} %param.10), kind=kOutput, calls=%fused_computation.23 | convolution fusion | flops 268435456 | bytes 3670016 | tf_op jit(solution)/shard_map/bij,bjv->biv/dot_general | solution.py:55
  41.9 1.1 convolution_bitcast_fusion.5
  43.9 9.3 %all-gather.1 = bf16[1024,16]{0,1:T(8,128)(2,1)S(1)} all-gather(bf16[256,16]{0,1:T(8,128)(2,1)} %reduce-scatter.4.cloned.1.call-done), channel_id=3, replica_groups=mesh['wide'=4,'narrow'=8] {'wide'}, dimensions={0}, use_global_device_ids=true | all-gather | bytes 40960 | tf_op jit(solution)/shard_map/all_gather | solution.py:82
  54.3 1.3 fusion.78
  55.6 15.1 %all_gather.29 = bf16[256,128]{0,1:T(8,128)(2,1)} all-gather(bf16[256,16]{0,1:T(8,128)(2,1)S(1)} %fusion.78), channel_id=1, replica_groups=mesh['wide'=4,'narrow'=8] {'narrow'}, dimensions={1}, use_global_device_ids=true | all-gather | bytes 73728 | tf_op jit(solution)/shard_map/all_gather | solution.py:89
  71.8 2.5 fusion.40
  74.3 3.4 %fusion.46 = f32[4,512,128]{1,2,0:T(8,128)} fusion(f32[4,512,128]{1,2,0:T(8,128)S(1)} %fusion.40, f32[4,512,128]{1,2,0:T(8,128)S(1)} %copy-done.7, bf16[4,512,128]{2,1,0:T(8,128)(2,1)S(1)} %bitcast.258, bf16[4,3,512,512]{3,2,1,0:T(8,128)(2,1)} %param.10), kind=kOutput, calls=%fused_computation.43 | convolution fusion | flops 268959744 | bytes 5767168 | tf_op jit(solution)/shard_map/bij,bjv->biv/dot_general | solution.py:52
  77.7 2.6 copy.31
  80.2 2.5 copy.32
  82.8 3.0 %fusion.130 = (bf16[2048,128]{0,1:T(8,128)(2,1)S(1)}, f32[2048,128]{0,1:T(8,128)}) fusion(f32[2048,128]{0,1:T(8,128)S(1)} %copy.33, f32[128]{0:T(128)S(1)} %copy-done.11, f32[2048,128]{0,1:T(8,128)} %copy.32, bf16[2048,256]{1,0:T(8,128)(2,1)S(1)} %copy-done, f32[128,256]{1,0:T(8,128)} %convolution_bitcast_fusion.5, bf16[256,128]{0,1:T(8,128)(2,1)} %all_gather.29, ...), kind=kOutput, calls=%fused_computation.133 | convolution fusion | flops 152109056 | bytes 5046784 | tf_op jit(solution)/shard_map/dot_general | solution.py:92
  87.6 2.9 %collective-permute-start.2 = (bf16[512,128]{0,1:T(8,128)(2,1)}, bf16[512,128]{0,1:T(8,128)(2,1)}, u32[]{:S(2)}, u32[]{:S(2)}) collective-permute-start(bf16[512,128]{0,1:T(8,128)(2,1)} %get-tuple-element.11), channel_id=1, source_target_pairs={{0,1},{1,2},{2,3},{3,4},{4,5},{5,6},{6,7},{7,8},{8,9},{9,10},{10,1... | collective-permute-start | bytes 393224 | tf_op jit(solution)/shard_map/ppermute | solution.py:18
  90.5 1.3 collective-permute-start.3
  91.8 16.6 %all-gather.2 = bf16[2048,128]{0,1:T(8,128)(2,1)S(1)} all-gather(bf16[256,128]{0,1:T(8,128)(2,1)} %bitcast.261), channel_id=4, replica_groups=mesh['wide'=4,'narrow'=8] {'narrow'}, dimensions={0}, use_global_device_ids=true | all-gather | bytes 589824 | tf_op jit(solution)/shard_map/all_gather | solution.py:67
  109.4 2.4 copy.50
  111.8 1.4 fusion.114
  113.2 3.4 %fusion.18 = f32[4,128,512]{2,1,0:T(8,128)} fusion(bf16[4,3,512,512]{3,2,1,0:T(8,128)(2,1)} %param.10, bf16[16,4,8,512]{3,2,1,0:T(8,128)(2,1)S(1)} %bitcast.245), kind=kOutput, calls=%fused_computation.21 | convolution fusion | flops 268435456 | bytes 3670016 | tf_op jit(solution)/shard_map/bij,bjv->biv/dot_general | solution.py:55
  117.6 11.4 %all-gather.3 = bf16[1024,16]{0,1:T(8,128)(2,1)} all-gather(bf16[256,16]{0,1:T(8,128)(2,1)} %reduce-scatter.6.cloned.1.call-done), channel_id=5, replica_groups=mesh['wide'=4,'narrow'=8] {'wide'}, dimensions={0}, use_global_device_ids=true | all-gather | bytes 40960 | tf_op jit(solution)/shard_map/all_gather | solution.py:82
  129.0 1.4 reshape.31
  130.4 1.6 fusion.123
  132.0 1.6 copy.52
  133.6 1.3 fusion.77
  134.9 15.1 %all_gather.32 = bf16[256,128]{0,1:T(8,128)(2,1)} all-gather(bf16[256,16]{0,1:T(8,128)(2,1)S(1)} %fusion.77), channel_id=1, replica_groups=mesh['wide'=4,'narrow'=8] {'narrow'}, dimensions={1}, use_global_device_ids=true | all-gather | bytes 73728 | tf_op jit(solution)/shard_map/all_gather | solution.py:89
  150.1 1.1 pad_maximum_fusion.3
  151.1 2.4 fusion.12
  153.6 2.4 fusion.55
  157.0 3.3 %fusion.133 = (bf16[2048,128]{0,1:T(8,128)(2,1)S(1)}, f32[2048,128]{0,1:T(8,128)}) fusion(f32[2048,128]{0,1:T(8,128)S(1)} %copy.33, f32[2048,128]{0,1:T(8,128)} %get-tuple-element.18, f32[128]{0:T(128)S(1)} %copy-done.11, f32[2048,128]{0,1:T(8,128)} %bitcast.247, bf16[2048,256]{1,0:T(8,128)(2,1)S(1)} %copy-done, f32[128,256]{1,0:T(8,128)} %convolution_bitcast_fusion.4, ...), kind=kOutput, calls=%fused_computation.134 | convolution fusion | flops 152633344 | bytes 6095360 | tf_op jit(solution)/shard_map/dot_general | solution.py:92
  162.2 2.9 %collective-permute-start.4 = (bf16[512,128]{0,1:T(8,128)(2,1)}, bf16[512,128]{0,1:T(8,128)(2,1)}, u32[]{:S(2)}, u32[]{:S(2)}) collective-permute-start(bf16[512,128]{0,1:T(8,128)(2,1)} %get-tuple-element.7), channel_id=1, source_target_pairs={{0,1},{1,2},{2,3},{3,4},{4,5},{5,6},{6,7},{7,8},{8,9},{9,10},{10,1... | collective-permute-start | bytes 393224 | tf_op jit(solution)/shard_map/ppermute | solution.py:18
  165.1 1.3 collective-permute-start.5
  166.4 16.2 %all-gather.4 = bf16[2048,128]{0,1:T(8,128)(2,1)S(1)} all-gather(bf16[256,128]{0,1:T(8,128)(2,1)S(1)} %bitcast.262), channel_id=6, replica_groups=mesh['wide'=4,'narrow'=8] {'narrow'}, dimensions={0}, use_global_device_ids=true | all-gather | bytes 589824 | tf_op jit(solution)/shard_map/all_gather | solution.py:67
  183.5 1.6 copy.53
  185.5 3.4 %fusion.16 = f32[4,128,512]{2,1,0:T(8,128)} fusion(bf16[4,3,512,512]{3,2,1,0:T(8,128)(2,1)} %param.10, bf16[16,4,8,512]{3,2,1,0:T(8,128)(2,1)S(1)} %bitcast.244), kind=kOutput, calls=%fused_computation.19 | convolution fusion | flops 268435456 | bytes 3670016 | tf_op jit(solution)/shard_map/bij,bjv->biv/dot_general | solution.py:55
  190.0 1.9 reduce-scatter.8.cloned.1.call-done
  191.8 9.2 %all-gather.5 = bf16[1024,16]{0,1:T(8,128)(2,1)S(1)} all-gather(bf16[256,16]{0,1:T(8,128)(2,1)} %reduce-scatter.8.cloned.1.call-done), channel_id=7, replica_groups=mesh['wide'=4,'narrow'=8] {'wide'}, dimensions={0}, use_global_device_ids=true | all-gather | bytes 40960 | tf_op jit(solution)/shard_map/all_gather | solution.py:82
  201.6 14.2 %all_gather.35 = bf16[256,128]{0,1:T(8,128)(2,1)S(1)} all-gather(bf16[256,16]{0,1:T(8,128)(2,1)S(1)} %fusion.76), channel_id=1, replica_groups=mesh['wide'=4,'narrow'=8] {'narrow'}, dimensions={1}, use_global_device_ids=true | all-gather | bytes 73728 | tf_op jit(solution)/shard_map/all_gather | solution.py:89
  215.8 1.2 pad_maximum_fusion.1
  217.0 2.4 fusion.10
  219.4 2.4 fusion.64
  222.8 3.2 %multiply_reduce_fusion = (f32[128]{0:T(128)S(1)}, f32[2048,128]{0,1:T(8,128)}) fusion(f32[2048,128]{0,1:T(8,128)S(1)} %copy-done.1, f32[2048,128]{0,1:T(8,128)} %get-tuple-element.20, f32[128]{0:T(128)S(1)} %copy-done.11, f32[2048,128]{0,1:T(8,128)} %bitcast.249, bf16[2048,256]{1,0:T(8,128)(2,1)S(1)} %copy-done, f32[128,256]{1,0:T(8,128)S(1)} %copy-done.9, ...), kind=kOutput, calls=%fused_computation.77 | convolution fusion | flops 152895360 | bytes 5571584 | tf_op jit(solution)/shard_map/dot_general | solution.py:92
  226.0 38.2 %psum.7 = f32[128]{0:T(128)S(1)} all-reduce(f32[128]{0:T(128)S(1)} %get-tuple-element.21), channel_id=1, replica_groups=mesh['wide'=4,'narrow'=8] {'wide','narrow'}, use_global_device_ids=true, to_apply=%region_4.0 | all-reduce | flops 128 | bytes 1024 | tf_op jit(solution)/shard_map/psum | solution.py:99
  264.3 1.4 broadcast_divide_fusion
  265.6 1.3 copy.43
  (64 shorter events, 15.1 us)
Async XLA Ops:
  6.5 1.5 copy-start
  6.5 30.4 %copy-start.10 = (s32[1,6]{1,0:T(1,128)S(1)}, s32[1,6]{1,0:T(1,128)}, u32[]{:S(2)}) copy-start(s32[1,6]{1,0:T(1,128)} %param.14) | copy-start | bytes 76
  6.5 35.3 %copy-start.2 = (bf16[1,6,256,256]{3,2,1,0:T(8,128)(2,1)S(1)}, bf16[1,6,256,256]{3,2,1,0:T(8,128)(2,1)}, u32[]{:S(2)}) copy-start(bf16[1,6,256,256]{3,2,1,0:T(8,128)(2,1)} %param.13) | copy-start | bytes 2359300
  6.5 46.7 %copy-start.12 = (s32[1,3]{1,0:T(1,128)S(1)}, s32[1,3]{1,0:T(1,128)}, u32[]{:S(2)}) copy-start(s32[1,3]{1,0:T(1,128)} %param.16) | copy-start | bytes 40
  6.5 37.3 %reduce-scatter.4.cloned.1.call-start = ((), (), s32[]{:S(2)}) async-start(), calls=%async_computation.3 | async-start | bytes 73728 | tf_op jit(solution)/shard_map/reduce_scatter | solution.py:78
  10.3 107.3 %reduce-scatter.6.cloned.1.call-start = ((), (), s32[]{:S(2)}) async-start(), calls=%async_computation.4 | async-start | bytes 73728 | tf_op jit(solution)/shard_map/reduce_scatter | solution.py:78
  11.1 59.6 %collective-permute-start = (bf16[512,128]{1,0:T(8,128)(2,1)}, bf16[512,128]{1,0:T(8,128)(2,1)}, u32[]{:S(2)}, u32[]{:S(2)}) collective-permute-start(bf16[512,128]{1,0:T(8,128)(2,1)} %get-tuple-element.15), channel_id=1, source_target_pairs={{0,1},{1,2},{2,3},{3,4},{4,5},{5,6},{6,7},{7,8},{8,9},{9,10},{10,1... | collective-permute-start | bytes 393224 | tf_op jit(solution)/shard_map/ppermute | solution.py:18
  14.1 56.6 %collective-permute-start.1 = (bf16[512,128]{1,0:T(8,128)(2,1)}, bf16[512,128]{1,0:T(8,128)(2,1)}, u32[]{:S(2)}, u32[]{:S(2)}) collective-permute-start(bf16[512,128]{1,0:T(8,128)(2,1)} %get-tuple-element.16), channel_id=1, source_target_pairs={{1,0},{2,1},{3,2},{4,3},{5,4},{6,5},{7,6},{8,7},{9,8},{10,9},{11,1... | collective-permute-start | bytes 393224 | tf_op jit(solution)/shard_map/ppermute | solution.py:20
  54.3 20.0 %copy-start.7 = (f32[4,512,128]{1,2,0:T(8,128)S(1)}, f32[4,512,128]{1,2,0:T(8,128)}, u32[]{:S(2)}) copy-start(f32[4,512,128]{1,2,0:T(8,128)} %fusion.20) | copy-start | bytes 3145732
  71.7 11.0 %copy-start.3 = (bf16[1,256,256]{2,1,0:T(8,128)(2,1)S(1)}, bf16[1,256,256]{2,1,0:T(8,128)(2,1)}, u32[]{:S(2)}) copy-start(bf16[1,256,256]{2,1,0:T(8,128)(2,1)} %param.12) | copy-start | bytes 393220
  71.7 11.0 %copy-start.11 = (f32[128]{0:T(128)S(1)}, f32[128]{0:T(128)}, u32[]{:S(2)}) copy-start(f32[128]{0:T(128)} %param.17) | copy-start | bytes 1540
  86.0 0.7 copy-start.8
  87.6 104.2 %reduce-scatter.8.cloned.1.call-start = ((), (), s32[]{:S(2)}) async-start(), calls=%async_computation.5 | async-start | bytes 73728 | tf_op jit(solution)/shard_map/reduce_scatter | solution.py:78
  87.6 62.4 %collective-permute-start.2 = (bf16[512,128]{0,1:T(8,128)(2,1)}, bf16[512,128]{0,1:T(8,128)(2,1)}, u32[]{:S(2)}, u32[]{:S(2)}) collective-permute-start(bf16[512,128]{0,1:T(8,128)(2,1)} %get-tuple-element.11), channel_id=1, source_target_pairs={{0,1},{1,2},{2,3},{3,4},{4,5},{5,6},{6,7},{7,8},{8,9},{9,10},{10,1... | collective-permute-start | bytes 393224 | tf_op jit(solution)/shard_map/ppermute | solution.py:18
  90.5 59.5 %collective-permute-start.3 = (bf16[512,128]{0,1:T(8,128)(2,1)}, bf16[512,128]{0,1:T(8,128)(2,1)}, u32[]{:S(2)}, u32[]{:S(2)}) collective-permute-start(bf16[512,128]{0,1:T(8,128)(2,1)} %get-tuple-element.12), channel_id=1, source_target_pairs={{1,0},{2,1},{3,2},{4,3},{5,4},{6,5},{7,6},{8,7},{9,8},{10,9},{11,1... | collective-permute-start | bytes 393224 | tf_op jit(solution)/shard_map/ppermute | solution.py:20
  133.6 20.0 %copy-start.4 = (f32[4,128,512]{2,1,0:T(8,128)S(1)}, f32[4,128,512]{2,1,0:T(8,128)}, u32[]{:S(2)}) copy-start(f32[4,128,512]{2,1,0:T(8,128)} %fusion.18) | copy-start | bytes 3145732
  160.3 41.1 %copy-start.6 = (bf16[1,3,256,256]{3,2,1,0:T(8,128)(2,1)S(1)}, bf16[1,3,256,256]{3,2,1,0:T(8,128)(2,1)}, u32[]{:S(2)}) copy-start(bf16[1,3,256,256]{3,2,1,0:T(8,128)(2,1)} %param.15) | copy-start | bytes 1179652
  162.2 53.6 %collective-permute-start.4 = (bf16[512,128]{0,1:T(8,128)(2,1)}, bf16[512,128]{0,1:T(8,128)(2,1)}, u32[]{:S(2)}, u32[]{:S(2)}) collective-permute-start(bf16[512,128]{0,1:T(8,128)(2,1)} %get-tuple-element.7), channel_id=1, source_target_pairs={{0,1},{1,2},{2,3},{3,4},{4,5},{5,6},{6,7},{7,8},{8,9},{9,10},{10,1... | collective-permute-start | bytes 393224 | tf_op jit(solution)/shard_map/ppermute | solution.py:18
  165.1 50.7 %collective-permute-start.5 = (bf16[512,128]{0,1:T(8,128)(2,1)}, bf16[512,128]{0,1:T(8,128)(2,1)}, u32[]{:S(2)}, u32[]{:S(2)}) collective-permute-start(bf16[512,128]{0,1:T(8,128)(2,1)} %get-tuple-element.8), channel_id=1, source_target_pairs={{1,0},{2,1},{3,2},{4,3},{5,4},{6,5},{7,6},{8,7},{9,8},{10,9},{11,1... | collective-permute-start | bytes 393224 | tf_op jit(solution)/shard_map/ppermute | solution.py:20
  201.4 17.9 %copy-start.5 = (f32[4,128,512]{2,1,0:T(8,128)S(1)}, f32[4,128,512]{2,1,0:T(8,128)}, u32[]{:S(2)}) copy-start(f32[4,128,512]{2,1,0:T(8,128)} %fusion.16) | copy-start | bytes 3145732
  215.8 7.0 %copy-start.1 = (f32[2048,128]{0,1:T(8,128)S(1)}, f32[2048,128]{0,1:T(8,128)}, u32[]{:S(2)}) copy-start(f32[2048,128]{0,1:T(8,128)} %get-tuple-element.18) | copy-start | bytes 3145732
  215.8 7.0 %copy-start.9 = (f32[128,256]{1,0:T(8,128)S(1)}, f32[128,256]{1,0:T(8,128)}, u32[]{:S(2)}) copy-start(f32[128,256]{1,0:T(8,128)} %convolution_bitcast_fusion.3) | copy-start | bytes 393220
Sparse Core Ops, SparseCore 0:
  10.4 33.3 reduce-scatter.3
  87.7 29.6 reduce-scatter.5
  162.3 29.4 reduce-scatter.7
where the time goes:
time: 275 us; the launch traced here: 273 us
  blocking collectives  165 us (60%)
  matrix products  50.8 us (18%)
  local copies, waits for them, and re-layouts  22.2 us (8%)
  between operations  13.4 us (5%)
  starting transfers between devices  12.8 us (5%)
  other arithmetic  6.05 us (2%)
  waiting for transfers between devices  2.84 us (1%)
    all_gather x3, blocking collectives, apply_operator(): lax.all_gather(coeff_b[None], 'narrow', axis=0, tiled=True)  52.9 us
    all_gather x3, blocking collectives, apply_operator(): parent_out = lax.all_gather(part_out, 'narrow', axis=1, tiled=True)  44.4 us
    psum x1, blocking collectives, shards(): squares = lax.psum(jnp.sum(current * current, axis=0), ('wide', 'narrow'))  38.2 us
    all_gather x3, blocking collectives, apply_operator(): lax.all_gather(top_in, 'wide', axis=0, tiled=True)  29.9 us
    dot_general x3, matrix products, apply_operator(): jnp.einsum('bij,bjv->biv', near_blocks[:, 1], fields[1:-1], preferred_ele...  10.2 us
    dot_general x3, matrix products, apply_operator(): jnp.dot(leaf_basis, far_coeff, preferred_element_type=jnp.float32)  9.46 us
    ppermute x3, starting transfers between devices, extended_2(): lax.ppermute(tail, axis, [(i, (i + 1) % count) for i in range(ends)])  8.8 us
    dot_general x3, matrix products, apply_operator(): jnp.einsum('bij,bjv->biv', near_blocks[:, 0], fields[:-2], preferred_elem...  8.21 us
  transfers between devices with their start and end apart: 9, of which 2 were waited for; matrix products, arithmetic and copies ran while one was open for 12% of the time, Pallas kernels for 0%

commit v1 on v0

v1 whole, which is shorter than its diff:
```python
import functools

import jax
import jax.numpy as jnp
from jax import lax
from jax.experimental import pallas as pl
from jax.experimental.pallas import tpu as pltpu
from jax.sharding import PartitionSpec as P

DEGREE = 3
MESH = pl.DeviceIdType.MESH


def nn(a, b):
    return jnp.dot(a, b, preferred_element_type=jnp.float32)


def nt(a, b):
    return lax.dot_general(a, b, (((1,), (1,)), ((), ())), preferred_element_type=jnp.float32)


def tn(a, b):
    return lax.dot_general(a, b, (((0,), (0,)), ((), ())), preferred_element_type=jnp.float32)


def await_bytes(ref, sem):
    pltpu.make_async_copy(ref, ref, sem).wait()


def find(partners, count, wanted):
    slot = jnp.int32(0)
    used = jnp.int32(0)
    for j in range(count):
        hit = partners[0, j] == wanted
        slot = jnp.where(hit, j, slot)
        used = jnp.where(hit, 1, used)
    return slot, used


def masked(values, used):
    return jnp.where(used > 0, values, jnp.zeros_like(values))


def kernel(
    wides, narrows,
    vec_hbm, near_hbm, basis_hbm, transfer_hbm, leafc_hbm, topc_hbm, leafp, topp, shift_ref,
    out_hbm, scale_ref,
    t, vin, acc, near_m, basis, basis_t, transfer, leafc, topc,
    coeffs, halo, up, shares, tops, outs, squares, sq_narrow, sq_wide,
    load_sem, ag_s, ag_r, fw_s, fw_r, halo_s, halo_r, rs_s, rs_r, top_s, top_r, out_s, out_r, sq_s, sq_r,
):
    w = lax.axis_index("wide")
    n = lax.axis_index("narrow")
    leaf = w * narrows + n
    leaves = wides * narrows
    sister = n + 1 - 2 * lax.rem(n, 2)
    chips = narrows // 2
    rows, columns = vec_hbm.shape
    rank = basis.shape[1]
    blocks, _, blk, _ = near_hbm.shape
    owners, sl = up.shape[1], up.shape[2]
    own = lax.rem(n, owners)
    group = (n // owners) * owners

    def send(src, dst, ssem, rsem, wi, ni):
        copy = pltpu.make_async_remote_copy(
            src_ref=src, dst_ref=dst, send_sem=ssem, recv_sem=rsem, device_id=(wi, ni), device_id_type=MESH
        )
        copy.start()

    loads = [
        pltpu.make_async_copy(vec_hbm, t.at[0], load_sem.at[0]),
        pltpu.make_async_copy(basis_hbm, basis, load_sem.at[1]),
        pltpu.make_async_copy(transfer_hbm, transfer, load_sem.at[2]),
        pltpu.make_async_copy(near_hbm, near_m, load_sem.at[3]),
        pltpu.make_async_copy(topc_hbm, topc, load_sem.at[4]),
        pltpu.make_async_copy(leafc_hbm, leafc, load_sem.at[5]),
    ]
    for load in loads:
        load.start()

    barrier = pltpu.get_barrier_semaphore()
    for d in range(1, narrows):
        pl.semaphore_signal(barrier, inc=1, device_id=(w, lax.rem(n + d, narrows)), device_id_type=MESH)
    for d in range(1, wides):
        pl.semaphore_signal(barrier, inc=1, device_id=(lax.rem(w + d, wides), n), device_id_type=MESH)

    @pl.when(jnp.logical_and(n == 0, w > 0))
    def _():
        pl.semaphore_signal(barrier, inc=1, device_id=(w - 1, narrows - 1), device_id_type=MESH)

    @pl.when(jnp.logical_and(n == narrows - 1, w < wides - 1))
    def _():
        pl.semaphore_signal(barrier, inc=1, device_id=(w + 1, 0), device_id_type=MESH)

    t[1] = jnp.zeros((rows, columns), jnp.float32)

    @pl.when(leaf == 0)
    def _():
        for k in range(DEGREE):
            halo[k, 0] = jnp.zeros((blk, columns), jnp.bfloat16)

    @pl.when(leaf == leaves - 1)
    def _():
        for k in range(DEGREE):
            halo[k, 1] = jnp.zeros((blk, columns), jnp.bfloat16)

    loads[0].wait()
    vin[...] = t[0].astype(jnp.bfloat16)
    loads[1].wait()
    for b in range(blocks):
        at = pl.ds(b * blk, blk)
        basis_t[:, at] = basis[at, :].T
    loads[2].wait()

    before = jnp.logical_and(n == 0, w > 0).astype(jnp.int32)
    after = jnp.logical_and(n == narrows - 1, w < wides - 1).astype(jnp.int32)
    pl.semaphore_wait(barrier, narrows - 1 + wides - 1 + before + after)

    shift = shift_ref[...]

    def step(k, carry):
        cur = lax.rem(k, 2)
        nxt = 1 - cur
        coeff = nn(basis_t[...], vin[...]).astype(jnp.bfloat16)
        coeffs[k, n] = coeff
        up[k] = tn(coeff, transfer[0]).astype(jnp.bfloat16).reshape(owners, sl, rank)
        for d in range(1, narrows):
            to = lax.rem(n + d, narrows)
            send(up.at[k, lax.rem(to, owners)], shares.at[k, d - 1], rs_s.at[k], rs_r.at[k], w, to)
        for d in range(1, chips):
            to = lax.rem(n + 2 * d, narrows)
            send(coeffs.at[k, n], coeffs.at[k, n], ag_s.at[k], ag_r.at[k, d - 1], w, to)
        send(coeffs.at[k, n], coeffs.at[k, n], ag_s.at[k], fw_r.at[k], w, sister)

        @pl.when(leaf < leaves - 1)
        def _():
            to = leaf + 1
            send(
                vin.at[pl.ds(rows - blk, blk)], halo.at[k, 0], halo_s.at[k, 0], halo_r.at[k, 0],
                to // narrows, lax.rem(to, narrows),
            )

        @pl.when(leaf > 0)
        def _():
            to = leaf - 1
            send(
                vin.at[pl.ds(0, blk)], halo.at[k, 1], halo_s.at[k, 1], halo_r.at[k, 1],
                to // narrows, lax.rem(to, narrows),
            )

        @pl.when(k == 0)
        def _():
            loads[3].wait()

        def near(b):
            total = nn(near_m[b, 1], vin[b * blk : (b + 1) * blk, :])
            if b > 0:
                total += nn(near_m[b, 0], vin[(b - 1) * blk : b * blk, :])
            if b < blocks - 1:
                total += nn(near_m[b, 2], vin[(b + 1) * blk : (b + 2) * blk, :])
            acc[b * blk : (b + 1) * blk, :] = total

        for b in range(blocks // 2):
            near(b)
        await_bytes(shares.at[k], rs_r.at[k])
        total = up[k, own].astype(jnp.float32)
        for d in range(narrows - 1):
            total += shares[k, d].astype(jnp.float32)
        tops[k, w] = total.astype(jnp.bfloat16)
        for d in range(1, wides):
            send(tops.at[k, w], tops.at[k, w], top_s.at[k], top_r.at[k], lax.rem(w + d, wides), n)
        for b in range(blocks // 2, blocks):
            near(b)

        @pl.when(k == 0)
        def _():
            loads[4].wait()

        await_bytes(tops.at[k, pl.ds(0, wides - 1)], top_r.at[k])
        part = jnp.zeros((sl, rank), jnp.float32)
        for d in range(1, wides):
            at = lax.rem(w + d, wides)
            slot, used = find(topp, topc.shape[1], at)
            part += nt(masked(tops[k, at], used), topc[0, slot])
        outs[k, own] = part.astype(jnp.bfloat16)
        for d in range(1, owners):
            to = group + lax.rem(own + d, owners)
            send(outs.at[k, own], outs.at[k, own], out_s.at[k], out_r.at[k], w, to)

        for d in range(1, chips):
            at = lax.rem(n - 2 * d + narrows, narrows)
            await_bytes(coeffs.at[k, at], ag_r.at[k, d - 1])
            send(coeffs.at[k, at], coeffs.at[k, at], fw_s.at[k], fw_r.at[k], w, sister)

        @pl.when(leaf > 0)
        def _():
            await_bytes(halo.at[k, 0], halo_r.at[k, 0])

        @pl.when(leaf < leaves - 1)
        def _():
            await_bytes(halo.at[k, 1], halo_r.at[k, 1])

        acc[0:blk, :] += nn(near_m[0, 0], halo[k, 0])
        acc[rows - blk : rows, :] += nn(near_m[blocks - 1, 2], halo[k, 1])

        @pl.when(k == 0)
        def _():
            loads[5].wait()

        await_bytes(coeffs.at[k, pl.ds(0, chips)], fw_r.at[k])
        far = jnp.zeros((rank, columns), jnp.float32)
        for d in range(1, narrows):
            at = lax.rem(n + d, narrows)
            slot, used = find(leafp, leafc.shape[1], at)
            far += nn(leafc[0, slot], masked(coeffs[k, at], used))
        await_bytes(outs.at[k, pl.ds(0, owners - 1)], out_r.at[k])
        far += nt(transfer[0], outs[k].reshape(columns, rank))
        far_b = far.astype(jnp.bfloat16)

        @pl.when(leaf < leaves - 1)
        def _():
            await_bytes(halo.at[k, 0], halo_s.at[k, 0])

        @pl.when(leaf > 0)
        def _():
            await_bytes(halo.at[k, 1], halo_s.at[k, 1])

        factor = jnp.where(k == 0, 1.0, 2.0)
        sums = jnp.zeros((8, columns), jnp.float32)
        for b in range(blocks):
            at = pl.ds(b * blk, blk)
            applied = acc[at, :] + nn(basis[at, :], far_b)
            fresh = factor * (applied - shift * t[cur, at, :]) - t[nxt, at, :]
            t[nxt, at, :] = fresh
            vin[at, :] = fresh.astype(jnp.bfloat16)
            sums += jnp.sum((fresh * fresh).reshape(blk // 8, 8, columns), axis=0)
        squares[0] = sums
        return carry

    lax.fori_loop(0, DEGREE, step, 0)

    result = pltpu.make_async_copy(t.at[DEGREE % 2], out_hbm, load_sem.at[6])
    result.start()
    for d in range(1, narrows):
        send(squares.at[0], sq_narrow.at[d - 1], sq_s.at[0], sq_r.at[0], w, lax.rem(n + d, narrows))
    await_bytes(sq_narrow, sq_r.at[0])
    total = squares[0]
    for d in range(narrows - 1):
        total += sq_narrow[d]
    squares[1] = total
    for d in range(1, wides):
        send(squares.at[1], sq_wide.at[d - 1], sq_s.at[1], sq_r.at[1], lax.rem(w + d, wides), n)

    for k in range(DEGREE):
        await_bytes(shares.at[k], rs_s.at[k])
        await_bytes(coeffs.at[k, pl.ds(0, chips)], ag_s.at[k])
        await_bytes(coeffs.at[k, pl.ds(0, chips - 1)], fw_s.at[k])
        await_bytes(tops.at[k, pl.ds(0, wides - 1)], top_s.at[k])
        await_bytes(outs.at[k, pl.ds(0, owners - 1)], out_s.at[k])
    await_bytes(sq_narrow, sq_s.at[0])
    await_bytes(sq_wide, sq_r.at[1])
    for d in range(wides - 1):
        total += sq_wide[d]
    mean = jnp.sum(total, axis=0, keepdims=True) / (rows * leaves)
    scale_ref[...] = jnp.sqrt(mean + 1e-06)
    await_bytes(sq_wide, sq_s.at[1])
    result.wait()


def shards(wides, narrows, vectors, near_blocks, leaf_basis, transfer, leaf_coupling, leaf_partners, parent_coupling, parent_partners, shifts):
    rows, columns = vectors.shape
    rank = leaf_basis.shape[1]
    blk = near_blocks.shape[2]
    sl = max(16, columns // narrows)
    owners = columns // sl
    bf16, f32 = jnp.bfloat16, jnp.float32
    dma = pltpu.SemaphoreType.DMA
    anywhere = pl.BlockSpec(memory_space=pl.ANY)
    scalars = pl.BlockSpec(memory_space=pltpu.SMEM)
    local = pl.BlockSpec(memory_space=pltpu.VMEM)
    raw, scale = pl.pallas_call(
        functools.partial(kernel, wides, narrows),
        out_shape=(
            jax.ShapeDtypeStruct((rows, columns), f32),
            jax.ShapeDtypeStruct((1, columns), f32),
        ),
        in_specs=[anywhere] * 6 + [scalars] * 2 + [local],
        out_specs=(anywhere, local),
        scratch_shapes=[
            pltpu.VMEM((2, rows, columns), f32),
            pltpu.VMEM((rows, columns), bf16),
            pltpu.VMEM((rows, columns), f32),
            pltpu.VMEM(near_blocks.shape, bf16),
            pltpu.VMEM((rows, rank), bf16),
            pltpu.VMEM((rank, rows), bf16),
            pltpu.VMEM(transfer.shape, bf16),
            pltpu.VMEM(leaf_coupling.shape, bf16),
            pltpu.VMEM(parent_coupling.shape, bf16),
            pltpu.VMEM((DEGREE, narrows, rank, columns), bf16),
            pltpu.VMEM((DEGREE, 2, blk, columns), bf16),
            pltpu.VMEM((DEGREE, owners, sl, rank), bf16),
            pltpu.VMEM((DEGREE, narrows - 1, sl, rank), bf16),
            pltpu.VMEM((DEGREE, wides, sl, rank), bf16),
            pltpu.VMEM((DEGREE, owners, sl, rank), bf16),
            pltpu.VMEM((2, 8, columns), f32),
            pltpu.VMEM((narrows - 1, 8, columns), f32),
            pltpu.VMEM((wides - 1, 8, columns), f32),
            dma((7,)),
            dma((DEGREE,)), dma((DEGREE, narrows // 2)),
            dma((DEGREE,)), dma((DEGREE,)),
            dma((DEGREE, 2)), dma((DEGREE, 2)),
            dma((DEGREE,)), dma((DEGREE,)),
            dma((DEGREE,)), dma((DEGREE,)),
            dma((DEGREE,)), dma((DEGREE,)),
            dma((2,)), dma((2,)),
        ],
        compiler_params=pltpu.CompilerParams(
            collective_id=0, has_side_effects=True, vmem_limit_bytes=56 * 1024 * 1024
        ),
    )(
        vectors, near_blocks, leaf_basis, transfer, leaf_coupling, parent_coupling,
        leaf_partners, parent_partners, shifts[None, :],
    )
    return raw / scale


def solution(mesh):
    return jax.shard_map(
        functools.partial(shards, mesh.shape["wide"], mesh.shape["narrow"]),
        mesh=mesh,
        in_specs=(
            P(("wide", "narrow"), None),
            P(("wide", "narrow"), None, None, None),
            P(("wide", "narrow"), None),
            P(("wide", "narrow"), None, None),
            P(("wide", "narrow"), None, None, None),
            P(("wide", "narrow"), None),
            P("wide", None, None, None),
            P("wide", None),
            P(),
        ),
        out_specs=P(("wide", "narrow"), None),
        check_vma=False,
    )
```

time: 275 us -> 59.8 us (0.22)
  blocking collectives: 165 us -> 0 us
  Pallas kernels: 0 us -> 57.4 us
  matrix products: 50.8 us -> 0 us
  local copies, waits for them, and re-layouts: 22.2 us -> 0 us
  between operations: 13.4 us -> 0.01 us
  starting transfers between devices: 12.8 us -> 0 us
  other arithmetic: 6.05 us -> 2.27 us
  waiting for transfers between devices: 2.84 us -> 0 us
    all_gather x9 -> x0, blocking collectives: 127 us -> none  [the longest x3 52.9 us: apply_operator(): lax.all_gather(coeff_b[None], 'narrow', axis=0, tiled=True)]
    pallas_call x0 -> x1, Pallas kernels: none -> 57.4 us  [shards(): pl.pallas_call(functools.partial(kernel, wides, narrows), out_shape=(jax....]
    dot_general x30 -> x0, matrix products: 50.8 us -> none  [the longest x3 10.2 us: apply_operator(): jnp.einsum('bij,bjv->biv', near_blocks[:, 1], fields[1:-1], preferred_ele...]
    psum x1 -> x0, blocking collectives: 38.2 us -> none  [shards(): squares = lax.psum(jnp.sum(current * current, axis=0), ('wide', 'narrow'))]
    ppermute x6 -> x0, starting transfers between devices: 12.6 us -> none  [the longest x3 8.8 us: extended_2(): lax.ppermute(tail, axis, [(i, (i + 1) % count) for i in range(ends)])]
    all_gather x5 -> x0, local copies, waits for them, and re-layouts: 5.43 us -> none  [the longest x2 4.01 us: apply_operator(): lax.all_gather(coeff_b[None], 'narrow', axis=0, tiled=True)]
    reshape x3 -> x0, local copies, waits for them, and re-layouts: 4.61 us -> none  [apply_operator(): near = near.reshape(local_rows, columns)]
    unnamed x29 -> x0, local copies, waits for them, and re-layouts: 3.52 us -> none
  transfers between devices with their start and end apart: 9 -> 0, of which waited for: 2 -> 0; matrix products, arithmetic and copies ran while one was open for 12% -> 0% of each run, Pallas kernels for 0% -> 0%
where the time goes in v1:
time: 59.8 us; the launch traced here: 59.7 us
  Pallas kernels  57.4 us (96%)
  other arithmetic  2.27 us (4%)
    pallas_call x1, Pallas kernels, shards(): pl.pallas_call(functools.partial(kernel, wides, narrows), out_shape=(jax....  57.4 us
    div x1, other arithmetic, shards(): return raw / scale  2.27 us

profile of v1, /device:TPU:0, one launch (start us, length us, event | category | flops | bytes accessed | tf_op | source)
XLA Modules:
  0.0 59.7 jit_solution(8278812576553267438)
XLA Ops:
  0.0 57.4 %shard_map.91 = (f32[2048,128]{1,0:T(8,128)}, f32[1,128]{1,0:T(1,128)}) custom-call(f32[2048,128]{1,0:T(8,128)} %vec_hbm.1, bf16[4,3,512,512]{3,2,1,0:T(8,128)(2,1)} %near_hbm.1, bf16[2048,256]{1,0:T(8,128)(2,1)} %basis_hbm.1, bf16[1,256,256]{2,1,0:T(8,128)(2,1)} %transfer_hbm.1, bf16[1,6,256,256]{3,2,1,0:T(8,128)(2,1)} %leafc_hbm.1, ...), custom_call_target="tpu_custom_call" | custom-call | tf_op jit(solution)/shard_map/pallas_call | solution.py:282
  57.4 2.3 %broadcast_divide_fusion = f32[2048,128]{1,0:T(8,128)} fusion(f32[2048,128]{1,0:T(8,128)} %get-tuple-element.7, f32[128]{0:T(128)} %bitcast.3), kind=kLoop, calls=%fused_computation | loop fusion | flops 262144 | bytes 2097664 | tf_op jit(solution)/shard_map/div | solution.py:325

commit v2 on v1

--- a/solution.py
+++ b/solution.py
@@ -45,7 +45,7 @@
     wides, narrows,
     vec_hbm, near_hbm, basis_hbm, transfer_hbm, leafc_hbm, topc_hbm, leafp, topp, shift_ref,
     out_hbm, scale_ref,
-    t, vin, acc, near_m, basis, basis_t, transfer, leafc, topc,
+    t, vin, acc, near_m, basis, basis_t, gram, transfer, leafc, topc,
     coeffs, halo, up, shares, tops, outs, squares, sq_narrow, sq_wide,
     load_sem, ag_s, ag_r, fw_s, fw_r, halo_s, halo_r, rs_s, rs_r, top_s, top_r, out_s, out_r, sq_s, sq_r,
 ):
@@ -93,8 +93,6 @@
     def _():
         pl.semaphore_signal(barrier, inc=1, device_id=(w + 1, 0), device_id_type=MESH)
 
-    t[1] = jnp.zeros((rows, columns), jnp.float32)
-
     @pl.when(leaf == 0)
     def _():
         for k in range(DEGREE):
@@ -119,10 +117,21 @@
 
     shift = shift_ref[...]
 
-    def step(k, carry):
-        cur = lax.rem(k, 2)
-        nxt = 1 - cur
-        coeff = nn(basis_t[...], vin[...]).astype(jnp.bfloat16)
+    def update(k, far_b):
+        sums = jnp.zeros((8, columns), jnp.float32)
+        for b in range(blocks):
+            at = pl.ds(b * blk, blk)
+            fresh = acc[at, :] + (1.0 if k == 1 else 2.0) * nn(basis[at, :], far_b)
+            t[k % 2, at, :] = fresh
+            if k < DEGREE:
+                vin[at, :] = fresh.astype(jnp.bfloat16)
+            else:
+                sums += jnp.sum((fresh * fresh).reshape(blk // 8, 8, columns), axis=0)
+        return sums
+
+    coeff = nn(basis_t[...], vin[...]).astype(jnp.bfloat16)
+    far_b = None
+    for k in range(DEGREE):
         coeffs[k, n] = coeff
         up[k] = tn(coeff, transfer[0]).astype(jnp.bfloat16).reshape(owners, sl, rank)
         for d in range(1, narrows):
@@ -132,6 +141,8 @@
             to = lax.rem(n + 2 * d, narrows)
             send(coeffs.at[k, n], coeffs.at[k, n], ag_s.at[k], ag_r.at[k, d - 1], w, to)
         send(coeffs.at[k, n], coeffs.at[k, n], ag_s.at[k], fw_r.at[k], w, sister)
+        if k > 0:
+            update(k, far_b)
 
         @pl.when(leaf < leaves - 1)
         def _():
@@ -149,8 +160,8 @@
                 to // narrows, lax.rem(to, narrows),
             )
 
-        @pl.when(k == 0)
-        def _():
+        if k == 0:
+            gram[...] = nn(basis_t[...], basis[...]).astype(jnp.bfloat16)
             loads[3].wait()
 
         def near(b):
@@ -173,8 +184,7 @@
         for b in range(blocks // 2, blocks):
             near(b)
 
-        @pl.when(k == 0)
-        def _():
+        if k == 0:
             loads[4].wait()
 
         await_bytes(tops.at[k, pl.ds(0, wides - 1)], top_r.at[k])
@@ -203,9 +213,17 @@
 
         acc[0:blk, :] += nn(near_m[0, 0], halo[k, 0])
         acc[rows - blk : rows, :] += nn(near_m[blocks - 1, 2], halo[k, 1])
-
-        @pl.when(k == 0)
-        def _():
+        local = jnp.zeros((rank, columns), jnp.float32)
+        for b in range(blocks):
+            at = pl.ds(b * blk, blk)
+            base = acc[at, :] - shift * t[k % 2, at, :]
+            if k > 0:
+                base = 2.0 * base - t[1 - k % 2, at, :]
+            acc[at, :] = base
+            if k < DEGREE - 1:
+                local += nn(basis_t[:, at], base.astype(jnp.bfloat16))
+
+        if k == 0:
             loads[5].wait()
 
         await_bytes(coeffs.at[k, pl.ds(0, chips)], fw_r.at[k])
@@ -226,20 +244,10 @@
         def _():
             await_bytes(halo.at[k, 1], halo_s.at[k, 1])
 
-        factor = jnp.where(k == 0, 1.0, 2.0)
-        sums = jnp.zeros((8, columns), jnp.float32)
-        for b in range(blocks):
-            at = pl.ds(b * blk, blk)
-            applied = acc[at, :] + nn(basis[at, :], far_b)
-            fresh = factor * (applied - shift * t[cur, at, :]) - t[nxt, at, :]
-            t[nxt, at, :] = fresh
-            vin[at, :] = fresh.astype(jnp.bfloat16)
-            sums += jnp.sum((fresh * fresh).reshape(blk // 8, 8, columns), axis=0)
-        squares[0] = sums
-        return carry
-
-    lax.fori_loop(0, DEGREE, step, 0)
-
+        if k < DEGREE - 1:
+            coeff = (local + (1.0 if k == 0 else 2.0) * nn(gram[...], far_b)).astype(jnp.bfloat16)
+
+    squares[0] = update(DEGREE, far_b)
     result = pltpu.make_async_copy(t.at[DEGREE % 2], out_hbm, load_sem.at[6])
     result.start()
     for d in range(1, narrows):
@@ -294,6 +302,7 @@
             pltpu.VMEM(near_blocks.shape, bf16),
             pltpu.VMEM((rows, rank), bf16),
             pltpu.VMEM((rank, rows), bf16),
+            pltpu.VMEM((rank, rank), bf16),
             pltpu.VMEM(transfer.shape, bf16),
             pltpu.VMEM(leaf_coupling.shape, bf16),
             pltpu.VMEM(parent_coupling.shape, bf16),

time: 59.8 us -> 58.4 us (0.977)
  Pallas kernels: 57.4 us -> 56 us
    pallas_call x1, Pallas kernels: 57.4 us -> 56 us  [shards(): pl.pallas_call(functools.partial(kernel, wides, narrows), out_shape=(jax....]
where the time goes in v2:
time: 58.4 us; the launch traced here: 58.3 us
  Pallas kernels  56 us (96%)
  other arithmetic  2.27 us (4%)
    pallas_call x1, Pallas kernels, shards(): pl.pallas_call(functools.partial(kernel, wides, narrows), out_shape=(jax....  56 us
    div x1, other arithmetic, shards(): return raw / scale  2.27 us

profile of v2, /device:TPU:0, one launch (start us, length us, event | category | flops | bytes accessed | tf_op | source)
XLA Modules:
  0.0 58.3 jit_solution(15379608533733324136)
XLA Ops:
  0.0 56.0 %shard_map.91 = (f32[2048,128]{1,0:T(8,128)}, f32[1,128]{1,0:T(1,128)}) custom-call(f32[2048,128]{1,0:T(8,128)} %vec_hbm.1, bf16[4,3,512,512]{3,2,1,0:T(8,128)(2,1)} %near_hbm.1, bf16[2048,256]{1,0:T(8,128)(2,1)} %basis_hbm.1, bf16[1,256,256]{2,1,0:T(8,128)(2,1)} %transfer_hbm.1, bf16[1,6,256,256]{3,2,1,0:T(8,128)(2,1)} %leafc_hbm.1, ...), custom_call_target="tpu_custom_call" | custom-call | tf_op jit(solution)/shard_map/pallas_call | solution.py:290
  56.0 2.3 %broadcast_divide_fusion = f32[2048,128]{1,0:T(8,128)} fusion(f32[2048,128]{1,0:T(8,128)} %get-tuple-element.7, f32[128]{0:T(128)} %bitcast.3), kind=kLoop, calls=%fused_computation | loop fusion | flops 262144 | bytes 2097664 | tf_op jit(solution)/shard_map/div | solution.py:334
